TPU v7x, 32 devices: a whole 2x2x4 slice. The times are simulated.
32 devices in a mesh: section: 8 (over y, x, core), dp: 4 (over z).
Axes of the slice: x: 2, y: 2, z: 4, core: 2. Of those that a mesh axis runs over, the one named last changes fastest.
Arguments:
- saved_x: bfloat16 [2, 3, 8, 4, 16, 16, 128], P(None, None, 'section', 'dp'), may hold values from -6 to 6
- saved_h: bfloat16 [2, 3, 8, 4, 16, 16, 128], P(None, None, 'section', 'dp'), may hold values from -6 to 6
- kernels: bfloat16 [8, 2, 2, 9, 128, 128], P('section'), as said below
- grad_in: bfloat16 [2, 8, 4, 16, 16, 128], P(None, 'section', 'dp'), may hold values from -6 to 6
- loss_grads: bfloat16 [2, 2, 4, 16, 16, 128], P(None, None, 'dp'), may hold values from -6 to 6
Outputs:
- kernel_grads: float32 [8, 2304, 128], P('section', 'dp')
- edge_grads: bfloat16 [2, 8, 4, 16, 16, 128], P(None, 'section', 'dp')
Inputs may be any that keep to these rules, and one draw needn't show every extreme that they name: kernels[d, 1] equals kernels[7 - d, 0]: each position holds replica 1's copy of the mirrored section. Every entry lies within 3 / sqrt(1152) in magnitude.
All inputs are finite; a program needn't handle non-finite values.
Results may differ from a plain program's by a relative error of at most 0.0052.
Values may be sent and summed in bfloat16 or wider, within the bound.
A program may use at most 64 MiB of HBM per device.

v0:
```python
import jax
import jax.numpy as jnp
from jax import lax
from jax.sharding import PartitionSpec as P


def from_behind(value, axis, by):
    peers = lax.axis_size(axis)
    pairs = [(i, i + by) for i in range(peers) if 0 <= i + by < peers]
    return lax.ppermute(value, axis, pairs)


def from_partner(value, axis, bit):
    mask = 2**bit
    pairs = [(source, source ^ mask) for source in range(lax.axis_size(axis))]
    return lax.ppermute(value, axis, pairs)


def tap_views(feature, sign):
    extent = feature.shape[1]
    padded = jnp.pad(feature, ((0, 0), (1, 1), (1, 1), (0, 0)))
    pieces = []
    for row_shift in (-1, 0, 1):
        for col_shift in (-1, 0, 1):
            row_start = 1 + sign * row_shift
            col_start = 1 + sign * col_shift
            pieces.append(
                padded[:, row_start : row_start + extent, col_start : col_start + extent, :]
            )
    return jnp.stack(pieces, axis=3)


def block_back(grad_out, inputs, hidden, w_first, w_second):
    act_h = jnp.maximum(hidden, 0)
    act_x = jnp.maximum(inputs, 0)
    grad_z = jnp.einsum(
        "byxkd,kcd->byxc", tap_views(grad_out, -1), w_second, preferred_element_type=jnp.float32
    )
    g_second = jnp.einsum(
        "byxkc,byxd->kcd", tap_views(act_h, 1), grad_out, preferred_element_type=jnp.float32
    )
    grad_h = jnp.where(hidden > 0, grad_z, 0.0).astype(jnp.bfloat16)
    grad_u = jnp.einsum(
        "byxkd,kcd->byxc", tap_views(grad_h, -1), w_first, preferred_element_type=jnp.float32
    )
    g_first = jnp.einsum(
        "byxkc,byxd->kcd", tap_views(act_x, 1), grad_h, preferred_element_type=jnp.float32
    )
    grad_x = (grad_out.astype(jnp.float32) + jnp.where(inputs > 0, grad_u, 0.0)).astype(
        jnp.bfloat16
    )
    return (grad_x, jnp.stack([g_first, g_second]))


def on_device(saved_x, saved_h, kernels, grad_in, loss_grads):
    position = lax.axis_index("section")
    sections_total = lax.axis_size("section")
    bit_count = sections_total.bit_length() - 1
    weights = kernels[0]
    ticks_total = saved_x.shape[1]
    incoming_a = grad_in[0, 0]
    incoming_b = grad_in[1, 0]
    total_a = None
    total_b = None
    for tick_index in range(ticks_total):
        if tick_index > 0:
            from_above = from_behind(out_a, "section", -1)
            from_below = from_behind(out_b, "section", 1)
            incoming_a = jnp.where(
                position == sections_total - 1, loss_grads[0, tick_index - 1], from_above
            )
            incoming_b = jnp.where(position == 0, loss_grads[1, tick_index - 1], from_below)
        out_a, grads_a = block_back(
            incoming_a,
            saved_x[0, tick_index, 0],
            saved_h[0, tick_index, 0],
            weights[0, 0],
            weights[0, 1],
        )
        out_b, grads_b = block_back(
            incoming_b,
            saved_x[1, tick_index, 0],
            saved_h[1, tick_index, 0],
            weights[1, 0],
            weights[1, 1],
        )
        total_a = grads_a if tick_index == 0 else total_a + grads_a
        total_b = grads_b if tick_index == 0 else total_b + grads_b
    channels = total_a.shape[-1]
    grad_a = total_a.reshape(-1, channels)
    grad_b = total_b.reshape(-1, channels)
    extent = saved_x.shape[4]
    factor = 1.0 / float(extent * extent)
    mirrored = grad_b
    for bit_number in range(bit_count):
        mirrored = from_partner(mirrored.astype(jnp.bfloat16), "section", bit_number).astype(
            mirrored.dtype
        )
    summed = lax.psum_scatter(grad_a + mirrored, "dp", scatter_dimension=0, tiled=True)
    kernel_grads = (summed * factor)[None]
    edge_grads = jnp.stack([out_a, out_b])[:, None]
    return (kernel_grads, edge_grads)


def solution(mesh):
    return jax.shard_map(
        on_device,
        mesh=mesh,
        in_specs=(
            P(None, None, "section", "dp", None, None, None),
            P(None, None, "section", "dp", None, None, None),
            P("section", None, None, None, None, None),
            P(None, "section", "dp", None, None, None),
            P(None, None, "dp", None, None, None),
        ),
        out_specs=(P("section", "dp", None), P(None, "section", "dp", None, None, None)),
        check_vma=False,
    )
```

profile of v0, /device:TPU:0, one launch (start us, length us, event | category | flops | bytes accessed | tf_op | source)
XLA Modules:
  0.0 132.9 jit_solution(1815050586442930822)
XLA Ops:
  7.2 0.9 slice_bitcast_fusion.24
  8.3 0.9 constant_dynamic-update-slice_fusion.112
  9.3 1.4 %fusion.25 = bf16[16,16,128]{2,1,0:T(8,128)(2,1)S(1)} fusion(bf16[1,16,16,9,128]{4,2,1,3,0:T(8,128)(2,1)S(1)} %constant_dynamic-update-slice_fusion.108, bf16[2,2,9,128,128]{4,3,2,1,0:T(8,128)(2,1)} %bitcast.1322, bf16[2,3,1,1,16,16,128]{6,5,4,3,2,1,0:T(8,128)(2,1)S(1)} %copy-done), kind=kOutput, calls=%fused_computation.52 | convolution fusion | flops 75595776 | bytes 1015808 | tf_op jit(solution)/shard_map/byxkd,kcd->byxc/dot_general | solution.py:36
  11.3 2.4 %collective-permute-start.2 = (bf16[1,16,16,128]{3,2,1,0:T(8,128)(2,1)S(1)}, bf16[1,16,16,128]{3,2,1,0:T(8,128)(2,1)S(1)}, u32[]{:S(2)}, u32[]{:S(2)}) collective-permute-start(bf16[1,16,16,128]{3,2,1,0:T(8,128)(2,1)S(1)} %fusion.30), channel_id=1, source_target_pairs={{0,4},{4,8},{8,12},{12,16},{16,20},{20,24},{24,28},{1,5},{5,9},{9,... | collective-permute-start | bytes 196616 | tf_op jit(solution)/shard_map/ppermute | solution.py:10
  14.8 1.3 collective-permute-start
  17.3 0.4 convolution_bitcast_fusion.10
  18.0 0.4 convolution_bitcast_fusion.4
  18.4 0.6 constant_dynamic-update-slice_fusion.156
  19.1 0.6 constant_dynamic-update-slice_fusion.155
  19.7 0.6 constant_dynamic-update-slice_fusion.154
  20.3 0.6 constant_dynamic-update-slice_fusion.170
  21.0 0.6 constant_dynamic-update-slice_fusion.169
  21.6 0.6 constant_dynamic-update-slice_fusion.168
  22.2 0.6 constant_dynamic-update-slice_fusion.167
  22.8 0.6 constant_dynamic-update-slice_fusion.107
  23.5 0.6 constant_dynamic-update-slice_fusion.106
  24.1 0.6 constant_dynamic-update-slice_fusion.105
  24.8 0.6 constant_dynamic-update-slice_fusion.104
  25.4 0.6 constant_dynamic-update-slice_fusion.71
  26.0 0.6 constant_dynamic-update-slice_fusion.70
  26.7 0.6 constant_dynamic-update-slice_fusion.69
  27.3 0.6 constant_dynamic-update-slice_fusion.68
  27.9 0.6 constant_dynamic-update-slice_fusion.35
  28.6 0.6 constant_dynamic-update-slice_fusion.34
  29.2 0.6 constant_dynamic-update-slice_fusion.33
  29.8 0.6 constant_dynamic-update-slice_fusion.32
  30.5 0.6 constant_dynamic-update-slice_fusion.8
  31.1 0.6 constant_dynamic-update-slice_fusion.7
  31.7 0.6 constant_dynamic-update-slice_fusion.6
  32.4 0.6 constant_dynamic-update-slice_fusion.5
  33.0 0.6 constant_dynamic-update-slice_fusion.134
  33.6 0.6 constant_dynamic-update-slice_fusion.133
  34.2 0.6 constant_dynamic-update-slice_fusion.132
  34.9 0.6 constant_dynamic-update-slice_fusion.131
  35.5 0.8 constant_dynamic-update-slice_fusion.166
  36.4 0.6 constant_dynamic-update-slice_fusion.3
  37.0 0.6 constant_dynamic-update-slice_fusion.2
  37.6 0.6 constant_dynamic-update-slice_fusion.1
  38.3 0.6 constant_dynamic-update-slice_fusion.30
  38.9 0.6 constant_dynamic-update-slice_fusion.29
  39.5 0.6 constant_dynamic-update-slice_fusion.28
  40.5 0.4 convolution_bitcast_fusion.5
  40.9 0.6 copy-done.5
  42.1 0.4 convolution_bitcast_fusion.2
  42.7 0.7 copy-done.13
  44.2 5.1 %collective-permute-start.3 = (bf16[1,16,16,128]{3,2,1,0:T(8,128)(2,1)S(1)}, bf16[1,16,16,128]{3,2,1,0:T(8,128)(2,1)S(1)}, u32[]{:S(2)}, u32[]{:S(2)}) collective-permute-start(bf16[1,16,16,128]{3,2,1,0:T(8,128)(2,1)S(1)} %add_convert_fusion.2), channel_id=1, source_target_pairs={{0,4},{4,8},{8,12},{12,16},{16,20},{20,24},{24,28},{1,5},{5,9},{9,... | collective-permute-start | bytes 196616 | tf_op jit(solution)/shard_map/ppermute | solution.py:10
  50.6 1.5 %collective-permute-start.1 = (bf16[1,16,16,128]{3,2,1,0:T(8,128)(2,1)S(1)}, bf16[1,16,16,128]{3,2,1,0:T(8,128)(2,1)S(1)}, u32[]{:S(2)}, u32[]{:S(2)}) collective-permute-start(bf16[1,16,16,128]{3,2,1,0:T(8,128)(2,1)S(1)} %add_convert_fusion.3), channel_id=1, source_target_pairs={{4,0},{8,4},{12,8},{16,12},{20,16},{24,20},{28,24},{5,1},{9,5},{13... | collective-permute-start | bytes 196616 | tf_op jit(solution)/shard_map/ppermute | solution.py:10
  52.0 0.4 convolution_bitcast_fusion.3
  52.4 2.5 %collective-permute-done.1 = bf16[1,16,16,128]{3,2,1,0:T(8,128)(2,1)S(1)} collective-permute-done((bf16[1,16,16,128]{3,2,1,0:T(8,128)(2,1)S(1)}, bf16[1,16,16,128]{3,2,1,0:T(8,128)(2,1)S(1)}, u32[]{:S(2)}, u32[]{:S(2)}) %collective-permute-start.1) | collective-permute-done | bytes 65568 | tf_op jit(solution)/shard_map/ppermute | solution.py:10
  55.0 0.4 convolution_bitcast_fusion
  56.8 3.0 %collective-permute-start.4 = (bf16[2304,128]{1,0:T(8,128)(2,1)S(1)}, bf16[2304,128]{1,0:T(8,128)(2,1)S(1)}, u32[]{:S(2)}, u32[]{:S(2)}) collective-permute-start(bf16[2304,128]{1,0:T(8,128)(2,1)S(1)} %bitcast.1321), channel_id=1, source_target_pairs={{0,4},{4,0},{8,12},{12,8},{16,20},{20,16},{24,28},{28,24},{1,5},{5... | collective-permute-start | bytes 1769480 | tf_op jit(solution)/shard_map/ppermute | solution.py:16
  59.8 0.4 convolution_bitcast_fusion.11
  60.1 0.4 convolution_bitcast_fusion.8
  60.5 0.4 convolution_bitcast_fusion.9
  60.9 0.5 collective-permute-done.4
  61.4 3.3 %collective-permute-start.5 = (bf16[2304,128]{1,0:T(8,128)(2,1)S(1)}, bf16[2304,128]{1,0:T(8,128)(2,1)S(1)}, u32[]{:S(2)}, u32[]{:S(2)}) collective-permute-start(bf16[2304,128]{1,0:T(8,128)(2,1)S(1)} %collective-permute-done.4), channel_id=1, source_target_pairs={{0,8},{4,12},{8,0},{12,4},{16,24},{20,28},{24,16},{28,20},{1,9},{5... | collective-permute-start | bytes 1769480 | tf_op jit(solution)/shard_map/ppermute | solution.py:16
  65.1 13.4 %collective-permute-done.5 = bf16[2304,128]{1,0:T(8,128)(2,1)S(1)} collective-permute-done((bf16[2304,128]{1,0:T(8,128)(2,1)S(1)}, bf16[2304,128]{1,0:T(8,128)(2,1)S(1)}, u32[]{:S(2)}, u32[]{:S(2)}) %collective-permute-start.5) | collective-permute-done | bytes 589856 | tf_op jit(solution)/shard_map/ppermute | solution.py:16
  78.8 0.4 convolution_bitcast_fusion.6
  79.2 0.4 convolution_bitcast_fusion.7
  79.8 13.8 %collective-permute-done.6 = bf16[2304,128]{1,0:T(8,128)(2,1)S(1)} collective-permute-done((bf16[2304,128]{1,0:T(8,128)(2,1)S(1)}, bf16[2304,128]{1,0:T(8,128)(2,1)S(1)}, u32[]{:S(2)}, u32[]{:S(2)}) %collective-permute-start.6) | collective-permute-done | bytes 589856 | tf_op jit(solution)/shard_map/ppermute | solution.py:16
  93.6 1.1 bitcast_add_fusion
  95.8 0.7 maximum_bitcast_fusion
  96.5 27.9 %reduce-scatter.2.cloned.1.call-done = f32[576,128]{1,0:T(8,128)} async-done(((f32[2304,128]{1,0:T(8,128)}), f32[576,128]{1,0:T(8,128)}) %reduce-scatter.2.cloned.1.call-update) | async-done | bytes 294928 | tf_op jit(solution)/shard_map/reduce_scatter | solution.py:99
  124.4 1.7 %multiply_bitcast_fusion = f32[1,576,128]{2,1,0:T(8,128)} fusion(f32[576,128]{1,0:T(8,128)} %reduce-scatter.2.cloned.1.call-done), kind=kLoop, calls=%fused_computation.304 | loop fusion | flops 73728 | bytes 589824 | tf_op jit(solution)/shard_map/broadcast_in_dim | solution.py:100
  (214 shorter events, 9.5 us)
Async XLA Ops:
  7.2 2.1 %copy-start = (bf16[2,3,1,1,16,16,128]{6,5,4,3,2,1,0:T(8,128)(2,1)S(1)}, bf16[2,3,1,1,16,16,128]{6,5,4,3,2,1,0:T(8,128)(2,1)}, u32[]{:S(2)}) copy-start(bf16[2,3,1,1,16,16,128]{6,5,4,3,2,1,0:T(8,128)(2,1)} %param.6) | copy-start | bytes 1179652
  7.2 117.2 %reduce-scatter.2.cloned.1.call-start = ((), (), s32[]{:S(2)}) async-start(), calls=%async_computation.1 | async-start | bytes 1474560 | tf_op jit(solution)/shard_map/reduce_scatter | solution.py:99
  9.2 1.7 %copy-start.1 = (bf16[2,3,1,1,16,16,128]{6,5,4,3,2,1,0:T(8,128)(2,1)S(1)}, bf16[2,3,1,1,16,16,128]{6,5,4,3,2,1,0:T(8,128)(2,1)}, u32[]{:S(2)}) copy-start(bf16[2,3,1,1,16,16,128]{6,5,4,3,2,1,0:T(8,128)(2,1)} %param.5) | copy-start | bytes 1179652
  9.2 1.7 %copy-start.2 = (bf16[2,1,1,16,16,128]{5,4,3,2,1,0:T(8,128)(2,1)S(1)}, bf16[2,1,1,16,16,128]{5,4,3,2,1,0:T(8,128)(2,1)}, u32[]{:S(2)}) copy-start(bf16[2,1,1,16,16,128]{5,4,3,2,1,0:T(8,128)(2,1)} %param.8) | copy-start | bytes 393220
  9.3 1.7 %copy-start.12 = (bf16[1,2,2,9,128,128]{5,4,3,2,1,0:T(8,128)(2,1)S(1)}, bf16[1,2,2,9,128,128]{5,4,3,2,1,0:T(8,128)(2,1)}, u32[]{:S(2)}) copy-start(bf16[1,2,2,9,128,128]{5,4,3,2,1,0:T(8,128)(2,1)} %param.7) | copy-start | bytes 3538948
  11.3 30.7 %collective-permute-start.2 = (bf16[1,16,16,128]{3,2,1,0:T(8,128)(2,1)S(1)}, bf16[1,16,16,128]{3,2,1,0:T(8,128)(2,1)S(1)}, u32[]{:S(2)}, u32[]{:S(2)}) collective-permute-start(bf16[1,16,16,128]{3,2,1,0:T(8,128)(2,1)S(1)} %fusion.30), channel_id=1, source_target_pairs={{0,4},{4,8},{8,12},{12,16},{16,20},{20,24},{24,28},{1,5},{5,9},{9,... | collective-permute-start | bytes 196616 | tf_op jit(solution)/shard_map/ppermute | solution.py:10
  14.8 27.2 %collective-permute-start = (bf16[1,16,16,128]{3,2,1,0:T(8,128)(2,1)S(1)}, bf16[1,16,16,128]{3,2,1,0:T(8,128)(2,1)S(1)}, u32[]{:S(2)}, u32[]{:S(2)}) collective-permute-start(bf16[1,16,16,128]{3,2,1,0:T(8,128)(2,1)S(1)} %fusion.29), channel_id=1, source_target_pairs={{4,0},{8,4},{12,8},{16,12},{20,16},{24,20},{28,24},{5,1},{9,5},{13... | collective-permute-start | bytes 196616 | tf_op jit(solution)/shard_map/ppermute | solution.py:10
  17.0 0.8 copy-start.4
  24.1 11.4 %copy-start.6 = (bf16[1,16,16,9,128]{4,2,1,3,0:T(8,128)(2,1)S(1)}, bf16[1,16,16,9,128]{4,2,1,3,0:T(8,128)(2,1)}, u32[]{:S(2)}) copy-start(bf16[1,16,16,9,128]{4,2,1,3,0:T(8,128)(2,1)} %constant_dynamic-update-slice_fusion.167) | copy-start | bytes 1769476
  25.4 10.1 %copy-start.7 = (bf16[1,16,16,9,128]{4,2,1,3,0:T(8,128)(2,1)S(1)}, bf16[1,16,16,9,128]{4,2,1,3,0:T(8,128)(2,1)}, u32[]{:S(2)}) copy-start(bf16[1,16,16,9,128]{4,2,1,3,0:T(8,128)(2,1)} %constant_dynamic-update-slice_fusion.104) | copy-start | bytes 1769476
  27.9 7.6 %copy-start.8 = (bf16[1,16,16,9,128]{4,2,1,3,0:T(8,128)(2,1)S(1)}, bf16[1,16,16,9,128]{4,2,1,3,0:T(8,128)(2,1)}, u32[]{:S(2)}) copy-start(bf16[1,16,16,9,128]{4,2,1,3,0:T(8,128)(2,1)} %constant_dynamic-update-slice_fusion.68) | copy-start | bytes 1769476
  36.3 4.0 %copy-start.11 = (bf16[1,16,16,9,128]{4,2,1,3,0:T(8,128)(2,1)S(1)}, bf16[1,16,16,9,128]{4,2,1,3,0:T(8,128)(2,1)}, u32[]{:S(2)}) copy-start(bf16[1,16,16,9,128]{4,2,1,3,0:T(8,128)(2,1)} %get-tuple-element.9) | copy-start | bytes 1769476
  40.5 1.1 copy-start.5
  40.5 1.2 copy-start.9
  40.5 1.4 %copy-start.10 = (bf16[1,16,16,9,128]{4,2,1,3,0:T(8,128)(2,1)S(1)}, bf16[1,16,16,9,128]{4,2,1,3,0:T(8,128)(2,1)}, u32[]{:S(2)}) copy-start(bf16[1,16,16,9,128]{4,2,1,3,0:T(8,128)(2,1)} %constant_dynamic-update-slice_fusion.1) | copy-start | bytes 1769476
  40.5 1.5 %copy-start.3 = (bf16[2,2,1,16,16,128]{5,4,3,2,1,0:T(8,128)(2,1)S(1)}, bf16[2,2,1,16,16,128]{5,4,3,2,1,0:T(8,128)(2,1)}, u32[]{:S(2)}) copy-start(bf16[2,2,1,16,16,128]{5,4,3,2,1,0:T(8,128)(2,1)} %param.9) | copy-start | bytes 786436
  42.1 1.3 copy-start.13
  44.2 8.2 %collective-permute-start.3 = (bf16[1,16,16,128]{3,2,1,0:T(8,128)(2,1)S(1)}, bf16[1,16,16,128]{3,2,1,0:T(8,128)(2,1)S(1)}, u32[]{:S(2)}, u32[]{:S(2)}) collective-permute-start(bf16[1,16,16,128]{3,2,1,0:T(8,128)(2,1)S(1)} %add_convert_fusion.2), channel_id=1, source_target_pairs={{0,4},{4,8},{8,12},{12,16},{16,20},{20,24},{24,28},{1,5},{5,9},{9,... | collective-permute-start | bytes 196616 | tf_op jit(solution)/shard_map/ppermute | solution.py:10
  50.6 4.4 %collective-permute-start.1 = (bf16[1,16,16,128]{3,2,1,0:T(8,128)(2,1)S(1)}, bf16[1,16,16,128]{3,2,1,0:T(8,128)(2,1)S(1)}, u32[]{:S(2)}, u32[]{:S(2)}) collective-permute-start(bf16[1,16,16,128]{3,2,1,0:T(8,128)(2,1)S(1)} %add_convert_fusion.3), channel_id=1, source_target_pairs={{4,0},{8,4},{12,8},{16,12},{20,16},{24,20},{28,24},{5,1},{9,5},{13... | collective-permute-start | bytes 196616 | tf_op jit(solution)/shard_map/ppermute | solution.py:10
  56.8 4.6 %collective-permute-start.4 = (bf16[2304,128]{1,0:T(8,128)(2,1)S(1)}, bf16[2304,128]{1,0:T(8,128)(2,1)S(1)}, u32[]{:S(2)}, u32[]{:S(2)}) collective-permute-start(bf16[2304,128]{1,0:T(8,128)(2,1)S(1)} %bitcast.1321), channel_id=1, source_target_pairs={{0,4},{4,0},{8,12},{12,8},{16,20},{20,16},{24,28},{28,24},{1,5},{5... | collective-permute-start | bytes 1769480 | tf_op jit(solution)/shard_map/ppermute | solution.py:16
  61.4 17.2 %collective-permute-start.5 = (bf16[2304,128]{1,0:T(8,128)(2,1)S(1)}, bf16[2304,128]{1,0:T(8,128)(2,1)S(1)}, u32[]{:S(2)}, u32[]{:S(2)}) collective-permute-start(bf16[2304,128]{1,0:T(8,128)(2,1)S(1)} %collective-permute-done.4), channel_id=1, source_target_pairs={{0,8},{4,12},{8,0},{12,4},{16,24},{20,28},{24,16},{28,20},{1,9},{5... | collective-permute-start | bytes 1769480 | tf_op jit(solution)/shard_map/ppermute | solution.py:16
  78.6 15.0 %collective-permute-start.6 = (bf16[2304,128]{1,0:T(8,128)(2,1)S(1)}, bf16[2304,128]{1,0:T(8,128)(2,1)S(1)}, u32[]{:S(2)}, u32[]{:S(2)}) collective-permute-start(bf16[2304,128]{1,0:T(8,128)(2,1)S(1)} %collective-permute-done.5), channel_id=1, source_target_pairs={{0,16},{4,20},{8,24},{12,28},{16,0},{20,4},{24,8},{28,12},{1,17},{... | collective-permute-start | bytes 1769480 | tf_op jit(solution)/shard_map/ppermute | solution.py:16
Sparse Core Ops, SparseCore 0:
  94.9 29.4 reduce-scatter.1
where the time goes:
time: 133 us
  waiting for transfers between devices  58.2 us (44%)
  local copies, waits for them, and re-layouts  28.6 us (22%)
  starting transfers between devices  16.9 us (13%)
  between operations  15.1 us (11%)
  matrix products  9.31 us (7%)
  other arithmetic  4.92 us (4%)
    reduce_scatter x1, waiting for transfers between devices, on_device(): lax.psum_scatter(grad_a + mirrored, 'dp', scatter_dimension=0, tiled=True)  27.9 us
    ppermute x3, waiting for transfers between devices, from_partner(): return lax.ppermute(value, axis, pairs)  27.8 us
    unnamed x208, local copies, waits for them, and re-layouts  27 us
    ppermute x4, starting transfers between devices, from_behind(): return lax.ppermute(value, axis, pairs)  10.3 us
    ppermute x3, starting transfers between devices, from_partner(): return lax.ppermute(value, axis, pairs)  6.58 us
    dot_general x6, matrix products, block_back(): jnp.einsum('byxkd,kcd->byxc', tap_views(grad_out, -1), w_second, preferre...  2.98 us
  transfers between devices with their start and end apart: 8, of which 5 were waited for; matrix products, arithmetic and copies ran while one was open for 23% of the time, Pallas kernels for 0%

commit v1 on v0

v1 whole, which is shorter than its diff:
```python
import functools

import jax
import jax.numpy as jnp
from jax import lax
from jax.experimental import pallas as pl
from jax.experimental.pallas import tpu as pltpu
from jax.sharding import PartitionSpec as P

MESH = pl.DeviceIdType.MESH
F32 = jnp.float32
BF16 = jnp.bfloat16


def dims(cfg):
    return cfg["S"], cfg["N"], cfg["T"], cfg["E"], cfg["C"]


def relay(cfg, x_hbm, h_hbm, w_hbm, g_hbm, l_hbm, kg_ref, edge_hbm,
          xs, hs, gs, ob, wc, vb, acc, rr, rl, sr, sl,
          in_sem, w_sem, l_sem, ms, mr, ts, tr, es, er, lsem, rs_s, rs_r, ls_s, ls_r):
    S, N, T, E, C = dims(cfg)
    M = E * E
    R = 18 * C // N
    me_s = lax.axis_index("section")
    me_p = lax.axis_index("dp")
    mirror = S - 1 - me_s
    first = me_s == 0
    last = me_s == S - 1

    local = {}
    local["g"] = pltpu.make_async_copy(g_hbm.at[0], gs.at[0, 0], in_sem.at[0])
    for t in range(T):
        local["h", t] = pltpu.make_async_copy(h_hbm.at[0, t], hs.at[t, 0], in_sem.at[1 + 2 * t])
        local["x", t] = pltpu.make_async_copy(x_hbm.at[0, t], xs.at[t, 0], in_sem.at[2 + 2 * t])
    weights = []
    for pair in range(2):
        weights.append([
            pltpu.make_async_copy(
                w_hbm.at[0, pair, k], wc.at[pair, :, pl.ds(k * C, C)], w_sem.at[pair, k])
            for k in range(9)
        ])
    losses = {
        (t, r): pltpu.make_async_copy(l_hbm.at[r, t - 1], gs.at[t, r], l_sem.at[t - 1, r])
        for t in range(1, T) for r in range(2)
    }
    local["g"].start()
    for c in weights[1]:
        c.start()
    local["h", 0].start()
    for c in weights[0]:
        c.start()
    local["x", 0].start()
    for t in range(1, T):
        local["h", t].start()
        local["x", t].start()

    @pl.when(last)
    def _():
        for c in losses.values():
            c.start()

    barrier = pltpu.get_barrier_semaphore()
    pl.semaphore_signal(barrier, inc=1, device_id=(mirror, me_p), device_id_type=MESH)

    @pl.when(me_s > 0)
    def _():
        pl.semaphore_signal(barrier, inc=1, device_id=(me_s - 1, me_p), device_id_type=MESH)

    @pl.when(me_s < S - 1)
    def _():
        pl.semaphore_signal(barrier, inc=1, device_id=(me_s + 1, me_p), device_id_type=MESH)

    @pl.when(me_p > 0)
    def _():
        pl.semaphore_signal(barrier, inc=1, device_id=(me_s, me_p - 1), device_id_type=MESH)

    @pl.when(me_p < N - 1)
    def _():
        pl.semaphore_signal(barrier, inc=1, device_id=(me_s, me_p + 1), device_id_type=MESH)

    greeted = (1 + (me_s > 0).astype(jnp.int32) + (me_s < S - 1).astype(jnp.int32)
               + (me_p > 0).astype(jnp.int32) + (me_p < N - 1).astype(jnp.int32))
    pl.semaphore_wait(barrier, greeted)

    def to_mirror(src, dst, i):
        return pltpu.make_async_remote_copy(
            src_ref=src, dst_ref=dst, send_sem=ms.at[i], recv_sem=mr.at[i],
            device_id=(mirror, me_p), device_id_type=MESH)

    moved = {"g": to_mirror(g_hbm.at[1], gs.at[0, 1], 0)}
    for t in range(T):
        moved["h", t] = to_mirror(h_hbm.at[1, t], hs.at[t, 1], 1 + 2 * t)
        moved["x", t] = to_mirror(x_hbm.at[1, t], xs.at[t, 1], 2 + 2 * t)
    for c in moved.values():
        c.start()

    steps = {
        (t, r): pltpu.make_async_remote_copy(
            src_ref=ob.at[t, r], dst_ref=gs.at[t + 1, r], send_sem=ts.at[t, r],
            recv_sem=tr.at[t, r], device_id=(me_s - 1, me_p), device_id_type=MESH)
        for t in range(T - 1) for r in range(2)
    }
    edge_home = pltpu.make_async_copy(ob.at[T - 1, 0], edge_hbm.at[0], lsem.at[0])
    edge_away = pltpu.make_async_remote_copy(
        src_ref=ob.at[T - 1, 1], dst_ref=edge_hbm.at[1], send_sem=es.at[0], recv_sem=er.at[0],
        device_id=(mirror, me_p), device_id_type=MESH)

    def right(q):
        return pltpu.make_async_remote_copy(
            src_ref=sr.at[q], dst_ref=rr.at[q], send_sem=rs_s.at[q], recv_sem=rs_r.at[q],
            device_id=(me_s, me_p + 1), device_id_type=MESH)

    def left(q):
        return pltpu.make_async_remote_copy(
            src_ref=sl.at[q], dst_ref=rl.at[q], send_sem=ls_s.at[q], recv_sem=ls_r.at[q],
            device_id=(me_s, me_p - 1), device_id_type=MESH)

    column = lax.broadcasted_iota(jnp.int32, (M, C), 0) % E
    low = column == 0
    high = column == E - 1
    for i in range(4):
        vb[i, 0:E, :] = jnp.zeros((E, 3 * C), BF16)
        vb[i, E + M:2 * E + M, :] = jnp.zeros((E, 3 * C), BF16)

    def spread(i, value):
        back = jnp.where(high, 0.0, pltpu.roll(value, M - 1, axis=0))
        ahead = jnp.where(low, 0.0, pltpu.roll(value, 1, axis=0))
        vb[i, E:E + M, 0:C] = back.astype(BF16)
        vb[i, E:E + M, C:2 * C] = value.astype(BF16)
        vb[i, E:E + M, 2 * C:3 * C] = ahead.astype(BF16)

    def rows(i, j):
        start = E - E * (j - 1)
        return vb[i, start:start + M, :]

    def conv(i, pair):
        total = None
        for j in range(3):
            part = lax.dot_general(
                rows(i, j), wc[pair, :, 3 * C * j:3 * C * (j + 1)],
                (((1,), (1,)), ((), ())), preferred_element_type=F32)
            total = part if total is None else total + part
        return total

    def weight_grad(i, pair, act, fresh):
        turned = jnp.maximum(act, 0).T
        for j in range(3):
            part = jnp.dot(turned, rows(i, j), preferred_element_type=F32)
            for d in range(3):
                at = (pair * 9 + 3 * j + d) * C
                piece = part[:, d * C:(d + 1) * C]
                if fresh:
                    acc[at:at + C, :] = piece
                else:
                    acc[at:at + C, :] += piece

    def own(q):
        return acc[q * R:(q + 1) * R, :]

    for t in range(T):
        for r in range(2):
            final = t == T - 1
            source = local if r == 0 else moved

            def arrived(name):
                if r == 0:
                    local[name].wait()
                else:
                    moved[name].wait_recv()

            if t == 0:
                arrived("g")
            else:
                @pl.when(last)
                def _():
                    losses[t, r].wait()

                @pl.when(jnp.logical_not(last))
                def _():
                    steps[t - 1, r].wait_recv()
            ga, gb = 2 * r, 2 * r + 1
            grad = gs[t, r].astype(F32)
            spread(ga, grad)
            if t == 0 and r == 0:
                for c in weights[1]:
                    c.wait()
            arrived(("h", t))
            hidden = hs[t, r]
            fresh = t == 0 and r == 0
            if final:
                weight_grad(ga, 1, hidden, fresh)
                if r == 1:
                    @pl.when(me_p == 0)
                    def _():
                        for q in range(N - 1, N // 2 - 1, -1):
                            if q > 0:
                                sr[q] = own(q).astype(BF16)
                                right(q).start()
            grad_h = jnp.where(hidden.astype(F32) > 0, conv(ga, 1), 0.0)
            spread(gb, grad_h)
            if t == 0 and r == 0:
                for c in weights[0]:
                    c.wait()
            arrived(("x", t))
            inputs = xs[t, r]
            if final:
                weight_grad(gb, 0, inputs, fresh)
                if r == 1:
                    @pl.when(me_p == 0)
                    def _():
                        for q in range(N // 2 - 1, 0, -1):
                            sr[q] = own(q).astype(BF16)
                            right(q).start()

                    @pl.when(me_p == N - 1)
                    def _():
                        for q in range(N - 1):
                            sl[q] = own(q).astype(BF16)
                            left(q).start()
            grad_u = conv(gb, 0)
            ob[t, r] = (grad + jnp.where(inputs.astype(F32) > 0, grad_u, 0.0)).astype(BF16)
            if final:
                if r == 0:
                    edge_home.start()
                else:
                    edge_away.start()
            else:
                @pl.when(me_s > 0)
                def _():
                    steps[t, r].start()

                weight_grad(ga, 1, hidden, fresh)
                weight_grad(gb, 0, inputs, fresh)

    inner = jnp.logical_and(me_p > 0, me_p < N - 1)
    for i in range(N - 1):
        up, down = N - 1 - i, i

        @pl.when(jnp.logical_and(inner, up > me_p))
        def _():
            right(up).wait_recv()
            sr[up] = (own(up) + rr[up].astype(F32)).astype(BF16)
            right(up).start()

        @pl.when(jnp.logical_and(inner, down < me_p))
        def _():
            left(down).wait_recv()
            sl[down] = (own(down) + rl[down].astype(F32)).astype(BF16)
            left(down).start()

    scale = 1.0 / float(E * E)
    for q in range(N):
        @pl.when(me_p == q)
        def _():
            total = own(q)
            if q > 0:
                right(q).wait_recv()
                total = total + rr[q].astype(F32)
            if q < N - 1:
                left(q).wait_recv()
                total = total + rl[q].astype(F32)
            kg_ref[...] = total * scale

    edge_home.wait()
    edge_away.wait()
    for c in moved.values():
        c.wait_send()

    @pl.when(me_s > 0)
    def _():
        for c in steps.values():
            c.wait_send()

    for q in range(N):
        @pl.when(q > me_p)
        def _():
            right(q).wait_send()

        @pl.when(q < me_p)
        def _():
            left(q).wait_send()


def on_device(saved_x, saved_h, kernels, grad_in, loss_grads):
    S, N = lax.axis_size("section"), lax.axis_size("dp")
    T, E, C = saved_x.shape[1], saved_x.shape[4], saved_x.shape[6]
    M = E * E * saved_x.shape[3]
    R = 18 * C // N
    cfg = dict(S=S, N=N, T=T, E=E, C=C)
    DMA = pltpu.SemaphoreType.DMA
    kg, edge = pl.pallas_call(
        functools.partial(relay, cfg),
        out_shape=(jax.ShapeDtypeStruct((R, C), F32), jax.ShapeDtypeStruct((2, M, C), BF16)),
        in_specs=[pl.BlockSpec(memory_space=pl.ANY)] * 5,
        out_specs=(pl.BlockSpec(memory_space=pltpu.VMEM), pl.BlockSpec(memory_space=pl.ANY)),
        scratch_shapes=[
            pltpu.VMEM((T, 2, M, C), BF16),
            pltpu.VMEM((T, 2, M, C), BF16),
            pltpu.VMEM((T, 2, M, C), BF16),
            pltpu.VMEM((T, 2, M, C), BF16),
            pltpu.VMEM((2, C, 9 * C), BF16),
            pltpu.VMEM((4, M + 2 * E, 3 * C), BF16),
            pltpu.VMEM((18 * C, C), F32),
            pltpu.VMEM((N, R, C), BF16),
            pltpu.VMEM((N, R, C), BF16),
            pltpu.VMEM((N, R, C), BF16),
            pltpu.VMEM((N, R, C), BF16),
            DMA((2 * T + 1,)),
            DMA((2, 9)),
            DMA((T, 2)),
            DMA((2 * T + 1,)),
            DMA((2 * T + 1,)),
            DMA((T, 2)),
            DMA((T, 2)),
            DMA((1,)),
            DMA((1,)),
            DMA((1,)),
            DMA((N,)),
            DMA((N,)),
            DMA((N,)),
            DMA((N,)),
        ],
        compiler_params=pltpu.CompilerParams(
            collective_id=0, has_side_effects=True, vmem_limit_bytes=40 * 1024 * 1024),
        cost_estimate=pl.CostEstimate(
            flops=48 * T * M * 9 * C * C // 6, bytes_accessed=3_000_000, transcendentals=0),
        name="relay",
    )(
        saved_x.reshape(2, T, M, C),
        saved_h.reshape(2, T, M, C),
        kernels.reshape(2, 2, 9, C, C),
        grad_in.reshape(2, M, C),
        loss_grads.reshape(2, T - 1, M, C),
    )
    return kg[None], edge.reshape(2, 1, 1, E, E, C)


def solution(mesh):
    return jax.shard_map(
        on_device,
        mesh=mesh,
        in_specs=(
            P(None, None, "section", "dp", None, None, None),
            P(None, None, "section", "dp", None, None, None),
            P("section", None, None, None, None, None),
            P(None, "section", "dp", None, None, None),
            P(None, None, "dp", None, None, None),
        ),
        out_specs=(P("section", "dp", None), P(None, "section", "dp", None, None, None)),
        check_vma=False,
    )
```

time: 133 us -> 48.3 us (0.36)
  waiting for transfers between devices: 58.2 us -> 0 us
  Pallas kernels: 0 us -> 40.9 us
  local copies, waits for them, and re-layouts: 28.6 us -> 6.48 us
  starting transfers between devices: 16.9 us -> 0 us
  between operations: 15.1 us -> 0.65 us
  matrix products: 9.31 us -> 0 us
  other arithmetic: 4.92 us -> 0 us
    pallas_call x0 -> x1, Pallas kernels: none -> 40.9 us  [on_device(): pl.pallas_call(functools.partial(relay, cfg), out_shape=(jax.ShapeDtypeSt...]
    ppermute x7 -> x0, waiting for transfers between devices: 30.3 us -> none  [the longest x3 27.8 us: from_partner(): return lax.ppermute(value, axis, pairs)]
    reduce_scatter x1 -> x0, waiting for transfers between devices: 27.9 us -> none  [on_device(): lax.psum_scatter(grad_a + mirrored, 'dp', scatter_dimension=0, tiled=True)]
    unnamed x208 -> x12, local copies, waits for them, and re-layouts: 27 us -> 6.48 us
    ppermute x7 -> x0, starting transfers between devices: 16.8 us -> none  [the longest x4 10.3 us: from_behind(): return lax.ppermute(value, axis, pairs)]
    dot_general x24 -> x0, matrix products: 9.31 us -> none  [the longest x6 2.98 us: block_back(): jnp.einsum('byxkd,kcd->byxc', tap_views(grad_out, -1), w_second, preferre...]
    broadcast_in_dim x1 -> x0, other arithmetic: 1.69 us -> none  [on_device(): kernel_grads = (summed * factor)[None]]
    unnamed x3 -> x0, other arithmetic: 1.54 us -> none
  transfers between devices with their start and end apart: 8 -> 0, of which waited for: 5 -> 0; matrix products, arithmetic and copies ran while one was open for 23% -> 0% of each run, Pallas kernels for 0% -> 0%
where the time goes in v1:
time: 48.3 us; the launch traced here: 48.1 us
  Pallas kernels  40.9 us (85%)
  local copies, waits for them, and re-layouts  6.48 us (13%)
  between operations  0.65 us (1%)
    pallas_call x1, Pallas kernels, on_device(): pl.pallas_call(functools.partial(relay, cfg), out_shape=(jax.ShapeDtypeSt...  40.9 us
    unnamed x12, local copies, waits for them, and re-layouts  6.48 us

profile of v1, /device:TPU:0, one launch (start us, length us, event | category | flops | bytes accessed | tf_op | source)
XLA Modules:
  0.0 48.1 jit_solution(17132918475375195104)
XLA Ops:
  0.6 0.0 copy-start
  0.6 1.3 %copy-done = bf16[1,2,2,9,128,128]{5,4,3,2,1,0:T(8,128)(2,1)S(1)} copy-done((bf16[1,2,2,9,128,128]{5,4,3,2,1,0:T(8,128)(2,1)S(1)}, bf16[1,2,2,9,128,128]{5,4,3,2,1,0:T(8,128)(2,1)}, u32[]{:S(2)}) %copy-start) | copy-done | bytes 1179672
  1.9 0.0 copy-start.1
  1.9 1.0 %copy-done.1 = bf16[2,3,1,1,16,16,128]{6,5,4,3,2,1,0:T(8,128)(2,1)S(1)} copy-done((bf16[2,3,1,1,16,16,128]{6,5,4,3,2,1,0:T(8,128)(2,1)S(1)}, bf16[2,3,1,1,16,16,128]{6,5,4,3,2,1,0:T(8,128)(2,1)}, u32[]{:S(2)}) %copy-start.1) | copy-done | bytes 393240
  2.9 0.0 copy-start.2
  2.9 1.0 %copy-done.2 = bf16[2,3,1,1,16,16,128]{6,5,4,3,2,1,0:T(8,128)(2,1)S(1)} copy-done((bf16[2,3,1,1,16,16,128]{6,5,4,3,2,1,0:T(8,128)(2,1)S(1)}, bf16[2,3,1,1,16,16,128]{6,5,4,3,2,1,0:T(8,128)(2,1)}, u32[]{:S(2)}) %copy-start.2) | copy-done | bytes 393240
  3.9 0.0 copy-start.3
  3.9 0.9 %copy-done.3 = bf16[2,2,1,16,16,128]{5,4,3,2,1,0:T(8,128)(2,1)S(1)} copy-done((bf16[2,2,1,16,16,128]{5,4,3,2,1,0:T(8,128)(2,1)S(1)}, bf16[2,2,1,16,16,128]{5,4,3,2,1,0:T(8,128)(2,1)}, u32[]{:S(2)}) %copy-start.3) | copy-done | bytes 262168
  4.8 0.0 copy-start.4
  4.8 0.9 %copy-done.4 = bf16[2,1,1,16,16,128]{5,4,3,2,1,0:T(8,128)(2,1)S(1)} copy-done((bf16[2,1,1,16,16,128]{5,4,3,2,1,0:T(8,128)(2,1)S(1)}, bf16[2,1,1,16,16,128]{5,4,3,2,1,0:T(8,128)(2,1)}, u32[]{:S(2)}) %copy-start.4) | copy-done | bytes 131096
  5.8 40.9 %relay.1 = (f32[576,128]{1,0:T(8,128)S(1)}, bf16[2,256,128]{2,1,0:T(8,128)(2,1)S(1)}) custom-call(bf16[2,3,256,128]{3,2,1,0:T(8,128)(2,1)S(1)} %bitcast.12, bf16[2,3,256,128]{3,2,1,0:T(8,128)(2,1)S(1)} %bitcast.13, bf16[2,2,9,128,128]{4,3,2,1,0:T(8,128)(2,1)S(1)} %bitcast.11, bf16[2,256,128]{2,1,0:T(8,128)(2,1)S(1)} %bitcast.15, ...), custom_call_target="tpu_custom_call" | custom-call | flops 905969664 | bytes 3000000 | tf_op jit(solution)/shard_map/relay/pallas_call | solution.py:292
  46.7 0.7 %copy.10 = f32[1,576,128]{2,1,0:T(8,128)} copy(f32[1,576,128]{2,1,0:T(8,128)S(1)} %bitcast.9) | data formatting | bytes 589824
  47.4 0.7 %copy.11 = bf16[2,1,1,16,16,128]{5,4,3,2,1,0:T(8,128)(2,1)} copy(bf16[2,1,1,16,16,128]{5,4,3,2,1,0:T(8,128)(2,1)S(1)} %bitcast.10) | data formatting | bytes 262144
Async XLA Ops:
  0.6 1.3 %copy-start = (bf16[1,2,2,9,128,128]{5,4,3,2,1,0:T(8,128)(2,1)S(1)}, bf16[1,2,2,9,128,128]{5,4,3,2,1,0:T(8,128)(2,1)}, u32[]{:S(2)}) copy-start(bf16[1,2,2,9,128,128]{5,4,3,2,1,0:T(8,128)(2,1)} %param.7) | copy-start | bytes 3538948
  1.9 1.0 %copy-start.1 = (bf16[2,3,1,1,16,16,128]{6,5,4,3,2,1,0:T(8,128)(2,1)S(1)}, bf16[2,3,1,1,16,16,128]{6,5,4,3,2,1,0:T(8,128)(2,1)}, u32[]{:S(2)}) copy-start(bf16[2,3,1,1,16,16,128]{6,5,4,3,2,1,0:T(8,128)(2,1)} %param.5) | copy-start | bytes 1179652
  2.9 1.0 %copy-start.2 = (bf16[2,3,1,1,16,16,128]{6,5,4,3,2,1,0:T(8,128)(2,1)S(1)}, bf16[2,3,1,1,16,16,128]{6,5,4,3,2,1,0:T(8,128)(2,1)}, u32[]{:S(2)}) copy-start(bf16[2,3,1,1,16,16,128]{6,5,4,3,2,1,0:T(8,128)(2,1)} %param.6) | copy-start | bytes 1179652
  3.9 0.9 %copy-start.3 = (bf16[2,2,1,16,16,128]{5,4,3,2,1,0:T(8,128)(2,1)S(1)}, bf16[2,2,1,16,16,128]{5,4,3,2,1,0:T(8,128)(2,1)}, u32[]{:S(2)}) copy-start(bf16[2,2,1,16,16,128]{5,4,3,2,1,0:T(8,128)(2,1)} %param.9) | copy-start | bytes 786436
  4.8 0.9 %copy-start.4 = (bf16[2,1,1,16,16,128]{5,4,3,2,1,0:T(8,128)(2,1)S(1)}, bf16[2,1,1,16,16,128]{5,4,3,2,1,0:T(8,128)(2,1)}, u32[]{:S(2)}) copy-start(bf16[2,1,1,16,16,128]{5,4,3,2,1,0:T(8,128)(2,1)} %param.8) | copy-start | bytes 393220

commit v2 on v1

--- a/solution.py
+++ b/solution.py
@@ -17,8 +17,8 @@
 
 
 def relay(cfg, x_hbm, h_hbm, w_hbm, g_hbm, l_hbm, kg_ref, edge_hbm,
-          xs, hs, gs, ob, wc, vb, acc, rr, rl, sr, sl,
-          in_sem, w_sem, l_sem, ms, mr, ts, tr, es, er, lsem, rs_s, rs_r, ls_s, ls_r):
+          xs, hs, gs, ob, wc, vb, acc, rr, sr,
+          in_sem, w_sem, l_sem, ms, mr, ts, tr, es, er, lsem, rs_s, rs_r):
     S, N, T, E, C = dims(cfg)
     M = E * E
     R = 18 * C // N
@@ -71,16 +71,12 @@
     def _():
         pl.semaphore_signal(barrier, inc=1, device_id=(me_s + 1, me_p), device_id_type=MESH)
 
-    @pl.when(me_p > 0)
-    def _():
-        pl.semaphore_signal(barrier, inc=1, device_id=(me_s, me_p - 1), device_id_type=MESH)
-
-    @pl.when(me_p < N - 1)
-    def _():
-        pl.semaphore_signal(barrier, inc=1, device_id=(me_s, me_p + 1), device_id_type=MESH)
-
-    greeted = (1 + (me_s > 0).astype(jnp.int32) + (me_s < S - 1).astype(jnp.int32)
-               + (me_p > 0).astype(jnp.int32) + (me_p < N - 1).astype(jnp.int32))
+    for q in range(N):
+        @pl.when(me_p != q)
+        def _():
+            pl.semaphore_signal(barrier, inc=1, device_id=(me_s, q), device_id_type=MESH)
+
+    greeted = N + (me_s > 0).astype(jnp.int32) + (me_s < S - 1).astype(jnp.int32)
     pl.semaphore_wait(barrier, greeted)
 
     def to_mirror(src, dst, i):
@@ -92,8 +88,15 @@
     for t in range(T):
         moved["h", t] = to_mirror(h_hbm.at[1, t], hs.at[t, 1], 1 + 2 * t)
         moved["x", t] = to_mirror(x_hbm.at[1, t], xs.at[t, 1], 2 + 2 * t)
-    for c in moved.values():
-        c.start()
+    groups = [["g", ("h", 0), ("x", 0)]] + [[("h", t), ("x", t)] for t in range(1, T)]
+
+    def send_group(t):
+        if t < T:
+            for name in groups[t]:
+                moved[name].start()
+
+    send_group(0)
+    send_group(1)
 
     steps = {
         (t, r): pltpu.make_async_remote_copy(
@@ -106,15 +109,15 @@
         src_ref=ob.at[T - 1, 1], dst_ref=edge_hbm.at[1], send_sem=es.at[0], recv_sem=er.at[0],
         device_id=(mirror, me_p), device_id_type=MESH)
 
-    def right(q):
+    def to_owner(q):
         return pltpu.make_async_remote_copy(
-            src_ref=sr.at[q], dst_ref=rr.at[q], send_sem=rs_s.at[q], recv_sem=rs_r.at[q],
-            device_id=(me_s, me_p + 1), device_id_type=MESH)
-
-    def left(q):
+            src_ref=sr.at[q], dst_ref=rr.at[me_p], send_sem=rs_s.at[q], recv_sem=rs_r.at[me_p],
+            device_id=(me_s, q), device_id_type=MESH)
+
+    def from_shard(p):
         return pltpu.make_async_remote_copy(
-            src_ref=sl.at[q], dst_ref=rl.at[q], send_sem=ls_s.at[q], recv_sem=ls_r.at[q],
-            device_id=(me_s, me_p - 1), device_id_type=MESH)
+            src_ref=sr.at[p], dst_ref=rr.at[p], send_sem=rs_s.at[p], recv_sem=rs_r.at[p],
+            device_id=(me_s, p), device_id_type=MESH)
 
     column = lax.broadcasted_iota(jnp.int32, (M, C), 0) % E
     low = column == 0
@@ -158,16 +161,20 @@
     def own(q):
         return acc[q * R:(q + 1) * R, :]
 
+    def send_sums(blocks):
+        for q in blocks:
+            @pl.when(me_p != q)
+            def _():
+                sr[q] = own(q).astype(BF16)
+                to_owner(q).start()
+
     for t in range(T):
         for r in range(2):
             final = t == T - 1
-            source = local if r == 0 else moved
 
             def arrived(name):
                 if r == 0:
                     local[name].wait()
-                else:
-                    moved[name].wait_recv()
 
             if t == 0:
                 arrived("g")
@@ -179,6 +186,10 @@
                 @pl.when(jnp.logical_not(last))
                 def _():
                     steps[t - 1, r].wait_recv()
+            if r == 1:
+                for name in groups[t]:
+                    moved[name].wait_recv()
+                send_group(t + 2)
             ga, gb = 2 * r, 2 * r + 1
             grad = gs[t, r].astype(F32)
             spread(ga, grad)
@@ -191,12 +202,7 @@
             if final:
                 weight_grad(ga, 1, hidden, fresh)
                 if r == 1:
-                    @pl.when(me_p == 0)
-                    def _():
-                        for q in range(N - 1, N // 2 - 1, -1):
-                            if q > 0:
-                                sr[q] = own(q).astype(BF16)
-                                right(q).start()
+                    send_sums(range(N // 2, N))
             grad_h = jnp.where(hidden.astype(F32) > 0, conv(ga, 1), 0.0)
             spread(gb, grad_h)
             if t == 0 and r == 0:
@@ -207,17 +213,7 @@
             if final:
                 weight_grad(gb, 0, inputs, fresh)
                 if r == 1:
-                    @pl.when(me_p == 0)
-                    def _():
-                        for q in range(N // 2 - 1, 0, -1):
-                            sr[q] = own(q).astype(BF16)
-                            right(q).start()
-
-                    @pl.when(me_p == N - 1)
-                    def _():
-                        for q in range(N - 1):
-                            sl[q] = own(q).astype(BF16)
-                            left(q).start()
+                    send_sums(range(N // 2))
             grad_u = conv(gb, 0)
             ob[t, r] = (grad + jnp.where(inputs.astype(F32) > 0, grad_u, 0.0)).astype(BF16)
             if final:
@@ -233,34 +229,16 @@
                 weight_grad(ga, 1, hidden, fresh)
                 weight_grad(gb, 0, inputs, fresh)
 
-    inner = jnp.logical_and(me_p > 0, me_p < N - 1)
-    for i in range(N - 1):
-        up, down = N - 1 - i, i
-
-        @pl.when(jnp.logical_and(inner, up > me_p))
-        def _():
-            right(up).wait_recv()
-            sr[up] = (own(up) + rr[up].astype(F32)).astype(BF16)
-            right(up).start()
-
-        @pl.when(jnp.logical_and(inner, down < me_p))
-        def _():
-            left(down).wait_recv()
-            sl[down] = (own(down) + rl[down].astype(F32)).astype(BF16)
-            left(down).start()
-
-    scale = 1.0 / float(E * E)
     for q in range(N):
         @pl.when(me_p == q)
         def _():
-            total = own(q)
-            if q > 0:
-                right(q).wait_recv()
-                total = total + rr[q].astype(F32)
-            if q < N - 1:
-                left(q).wait_recv()
-                total = total + rl[q].astype(F32)
-            kg_ref[...] = total * scale
+            kg_ref[...] = own(q)
+    for p in range(N):
+        @pl.when(me_p != p)
+        def _():
+            from_shard(p).wait_recv()
+            kg_ref[...] += rr[p].astype(F32)
+    kg_ref[...] *= 1.0 / float(E * E)
 
     edge_home.wait()
     edge_away.wait()
@@ -273,13 +251,9 @@
             c.wait_send()
 
     for q in range(N):
-        @pl.when(q > me_p)
+        @pl.when(me_p != q)
         def _():
-            right(q).wait_send()
-
-        @pl.when(q < me_p)
-        def _():
-            left(q).wait_send()
+            to_owner(q).wait_send()
 
 
 def on_device(saved_x, saved_h, kernels, grad_in, loss_grads):
@@ -292,8 +266,8 @@
     kg, edge = pl.pallas_call(
         functools.partial(relay, cfg),
         out_shape=(jax.ShapeDtypeStruct((R, C), F32), jax.ShapeDtypeStruct((2, M, C), BF16)),
-        in_specs=[pl.BlockSpec(memory_space=pl.ANY)] * 5,
-        out_specs=(pl.BlockSpec(memory_space=pltpu.VMEM), pl.BlockSpec(memory_space=pl.ANY)),
+        in_specs=[pl.BlockSpec(memory_space=pltpu.HBM)] * 5,
+        out_specs=(pl.BlockSpec(memory_space=pltpu.VMEM), pl.BlockSpec(memory_space=pltpu.HBM)),
         scratch_shapes=[
             pltpu.VMEM((T, 2, M, C), BF16),
             pltpu.VMEM((T, 2, M, C), BF16),
@@ -302,8 +276,6 @@
             pltpu.VMEM((2, C, 9 * C), BF16),
             pltpu.VMEM((4, M + 2 * E, 3 * C), BF16),
             pltpu.VMEM((18 * C, C), F32),
-            pltpu.VMEM((N, R, C), BF16),
-            pltpu.VMEM((N, R, C), BF16),
             pltpu.VMEM((N, R, C), BF16),
             pltpu.VMEM((N, R, C), BF16),
             DMA((2 * T + 1,)),
@@ -318,11 +290,9 @@
             DMA((1,)),
             DMA((N,)),
             DMA((N,)),
-            DMA((N,)),
-            DMA((N,)),
         ],
         compiler_params=pltpu.CompilerParams(
-            collective_id=0, has_side_effects=True, vmem_limit_bytes=40 * 1024 * 1024),
+            collective_id=0, has_side_effects=True, vmem_limit_bytes=63 * 1024 * 1024),
         cost_estimate=pl.CostEstimate(
             flops=48 * T * M * 9 * C * C // 6, bytes_accessed=3_000_000, transcendentals=0),
         name="relay",

time: 48.3 us -> 39.1 us (0.81)
  the two profiles are of different devices: /device:TPU:0 before, /device:TPU:9 now
where the time goes in v2:
time: 39.1 us; the launch traced here: 38.9 us
  Pallas kernels  35 us (90%)
  local copies, waits for them, and re-layouts  3.26 us (8%)
  between operations  0.64 us (2%)
    pallas_call x1, Pallas kernels, on_device(): pl.pallas_call(functools.partial(relay, cfg), out_shape=(jax.ShapeDtypeSt...  35 us
    unnamed x2, local copies, waits for them, and re-layouts  3.26 us

profile of v2, /device:TPU:9, one launch (start us, length us, event | category | flops | bytes accessed | tf_op | source)
XLA Modules:
  0.0 38.9 jit_solution(2229566373377258583)
XLA Ops:
  0.6 35.0 %relay.1 = (f32[576,128]{1,0:T(8,128)}, bf16[2,256,128]{2,1,0:T(8,128)(2,1)}) custom-call(bf16[2,3,256,128]{3,2,1,0:T(8,128)(2,1)} %bitcast.12, bf16[2,3,256,128]{3,2,1,0:T(8,128)(2,1)} %bitcast.13, bf16[2,2,9,128,128]{4,3,2,1,0:T(8,128)(2,1)} %bitcast.11, bf16[2,256,128]{2,1,0:T(8,128)(2,1)} %bitcast.15, bf16[2,2,256,128]{3,2,1,0:T(8,128)(2,1)} %bitcast.14), custom_call_target="tpu_custom_call" | custom-call | flops 905969664 | bytes 3000000 | tf_op jit(solution)/shard_map/relay/pallas_call | solution.py:266
  35.6 1.7 %copy.10 = f32[1,576,128]{2,1,0:T(8,128)} copy(f32[1,576,128]{2,1,0:T(8,128)} %bitcast.9) | data formatting | bytes 589824
  37.3 1.6 %copy.11 = bf16[2,1,1,16,16,128]{5,4,3,2,1,0:T(8,128)(2,1)} copy(bf16[2,1,1,16,16,128]{5,4,3,2,1,0:T(8,128)(2,1)} %bitcast.10) | data formatting | bytes 262144

commit v3 on v2

--- a/solution.py
+++ b/solution.py
@@ -168,8 +168,8 @@
                 sr[q] = own(q).astype(BF16)
                 to_owner(q).start()
 
-    for t in range(T):
-        for r in range(2):
+    for n in range(T + 1):
+        for t, r in [c for c in ((n, 0), (n - 1, 1)) if 0 <= c[0] < T]:
             final = t == T - 1
 
             def arrived(name):
@@ -229,16 +229,12 @@
                 weight_grad(ga, 1, hidden, fresh)
                 weight_grad(gb, 0, inputs, fresh)
 
-    for q in range(N):
-        @pl.when(me_p == q)
-        def _():
-            kg_ref[...] = own(q)
-    for p in range(N):
-        @pl.when(me_p != p)
-        def _():
-            from_shard(p).wait_recv()
-            kg_ref[...] += rr[p].astype(F32)
-    kg_ref[...] *= 1.0 / float(E * E)
+    total = acc[pl.ds(pl.multiple_of(me_p * R, R), R), :]
+    for k in range(1, N):
+        p = lax.rem(me_p + k, N)
+        from_shard(p).wait_recv()
+        total = total + rr[p].astype(F32)
+    kg_ref[...] = total * (1.0 / float(E * E))
 
     edge_home.wait()
     edge_away.wait()

time: 39.1 us -> 39 us (level)
  the two profiles are of different devices: /device:TPU:9 before, /device:TPU:11 now
where the time goes in v3:
time: 39 us; the launch traced here: 38.8 us
  Pallas kernels  34.9 us (89%)
  local copies, waits for them, and re-layouts  3.26 us (8%)
  between operations  0.64 us (2%)
    pallas_call x1, Pallas kernels, on_device(): pl.pallas_call(functools.partial(relay, cfg), out_shape=(jax.ShapeDtypeSt...  34.9 us
    unnamed x2, local copies, waits for them, and re-layouts  3.26 us

profile of v3, /device:TPU:11, one launch (start us, length us, event | category | flops | bytes accessed | tf_op | source)
XLA Modules:
  0.0 38.8 jit_solution(8172026137400736164)
XLA Ops:
  0.6 34.9 %relay.1 = (f32[576,128]{1,0:T(8,128)}, bf16[2,256,128]{2,1,0:T(8,128)(2,1)}) custom-call(bf16[2,3,256,128]{3,2,1,0:T(8,128)(2,1)} %bitcast.12, bf16[2,3,256,128]{3,2,1,0:T(8,128)(2,1)} %bitcast.13, bf16[2,2,9,128,128]{4,3,2,1,0:T(8,128)(2,1)} %bitcast.11, bf16[2,256,128]{2,1,0:T(8,128)(2,1)} %bitcast.15, bf16[2,2,256,128]{3,2,1,0:T(8,128)(2,1)} %bitcast.14), custom_call_target="tpu_custom_call" | custom-call | flops 905969664 | bytes 3000000 | tf_op jit(solution)/shard_map/relay/pallas_call | solution.py:262
  35.6 1.7 %copy.10 = f32[1,576,128]{2,1,0:T(8,128)} copy(f32[1,576,128]{2,1,0:T(8,128)} %bitcast.9) | data formatting | bytes 589824
  37.3 1.6 %copy.11 = bf16[2,1,1,16,16,128]{5,4,3,2,1,0:T(8,128)(2,1)} copy(bf16[2,1,1,16,16,128]{5,4,3,2,1,0:T(8,128)(2,1)} %bitcast.10) | data formatting | bytes 262144
